TPU v7x, 512 devices: a whole 4x8x8 slice. The times are simulated.
512 devices in a mesh: row: 16 (over y, core), col: 32 (over z, x).
Axes of the slice: x: 4, y: 8, z: 8, core: 2. Of those that a mesh axis runs over, the one named last changes fastest.
Arguments:
- matrix: float32 [16384, 16384], P('row', 'col'), may hold values from -24 to 24
- panel: float32 [16384, 256], P(('row', 'col')), may hold values from -21 to 21
Outputs:
- updated: float32 [16384, 16384], P('row', 'col')
All inputs are finite; a program needn't handle non-finite values.
Results may differ from a plain program's by a relative error of at most 0.0003.
Values sent between devices are 32-bit elements; how exact they have to be, the bound alone decides.
A program may use at most 64 MiB of HBM per device.

v0:
```python
import jax
import jax.numpy as jnp
from jax import lax
from jax.sharding import PartitionSpec as P

HIGH = lax.Precision.HIGHEST


def from_root(x, axis, root):
    mine = lax.axis_index(axis) == root
    return lax.psum(jnp.where(mine, x, jnp.zeros_like(x)), axis)


def mult(left, right):
    return jnp.dot(left, right, precision=HIGH, preferred_element_type=jnp.float32)


def on_device(matrix, panel):
    row_count = lax.axis_size("row")
    col_count = lax.axis_size("col")
    row_index = lax.axis_index("row")
    col_index = lax.axis_index("col")
    ratio = col_count // row_count
    local_rows = matrix.shape[0]
    local_cols = matrix.shape[1]
    gram = lax.psum(mult(panel.T, panel), ("row", "col"))
    factor = jnp.linalg.cholesky(gram)
    basis = jax.scipy.linalg.solve_triangular(factor, panel.T, lower=True).T
    basis_r = lax.all_gather(basis, "col", axis=0, tiled=True)
    offset = col_index % ratio * local_cols
    owner = col_index // ratio
    basis_half = lax.dynamic_slice_in_dim(basis_r, offset, local_cols, 0)
    basis_c = from_root(basis_half, "row", owner)
    product_part = lax.psum_scatter(mult(matrix, basis_c), "col", scatter_dimension=0, tiled=True)
    inner = lax.psum(mult(basis.T, product_part), ("row", "col"))
    shifted_part = product_part - 0.5 * mult(basis, inner)
    shifted_r = lax.all_gather(shifted_part, "col", axis=0, tiled=True)
    shifted_half = lax.dynamic_slice_in_dim(shifted_r, offset, local_cols, 0)
    shifted_c = from_root(shifted_half, "row", owner)
    row_ids = row_index * local_rows + jnp.arange(local_rows, dtype=jnp.int32)
    col_ids = col_index * local_cols + jnp.arange(local_cols, dtype=jnp.int32)
    lower = row_ids[:, None] >= col_ids[None, :]
    change = mult(basis_r, shifted_c.T) + mult(shifted_r, basis_c.T)
    return jnp.where(lower, matrix - change, matrix)


def solution(mesh):
    return jax.shard_map(
        on_device,
        mesh=mesh,
        in_specs=(P("row", "col"), P(("row", "col"), None)),
        out_specs=P("row", "col"),
        check_vma=False,
    )
```

profile of v0, /device:TPU:1, one launch (start us, length us, event | category | flops | bytes accessed | tf_op | source)
XLA Modules:
  0.0 1246.3 jit_solution(17668871432151546376)
XLA Ops:
  6.5 1.9 fusion.14
  8.6 276.6 %all-reduce.6.cloned.1.call-done = f32[256,256]{0,1:T(8,128)} async-done(((f32[256,256]{0,1:T(8,128)}), f32[256,256]{0,1:T(8,128)}) %all-reduce.6.cloned.1.call-update) | async-done | bytes 262160 | tf_op jit(solution)/shard_map/psum | solution.py:26
  285.2 1.1 copy.4
  286.2 1.0 fusion.1
  287.2 11.7 cholesky.50
  299.0 9.8 custom-call.15
  309.3 11.7 cholesky.105
  323.0 4.0 while.1
  323.8 1.3 bitcast_dynamic-update-slice_fusion.2
  325.7 1.3 bitcast_dynamic-update-slice_fusion.2
  327.0 19.7 %custom-call.16 = f32[2,128,128]{1,2,0:T(8,128)S(1)} custom-call(f32[2,128,128]{2,1,0:T(8,128)S(1)} %get-tuple-element.12), custom_call_target="InvertDiagBlocksLowerTriangular" | custom-call | tf_op jit(solution)/shard_map/jit(_solve_triangular)/triangular_solve | solution.py:28
  348.0 74.1 %all-gather.3.cloned.1.call-done = f32[1024,256]{1,0:T(8,128)} async-done(((f32[32,256]{1,0:T(8,128)}), f32[1024,256]{1,0:T(8,128)}) %all-gather.3.cloned.1.call-update) | async-done | bytes 1048592 | tf_op jit(solution)/shard_map/all_gather | solution.py:29
  422.1 1.9 dynamic-slice_select_fusion.1
  424.1 117.1 %all-reduce.8.cloned.1.call-done = f32[512,256]{1,0:T(8,128)} async-done(((f32[512,256]{1,0:T(8,128)}), f32[512,256]{1,0:T(8,128)}) %all-reduce.8.cloned.1.call-update) | async-done | bytes 524304 | tf_op jit(solution)/shard_map/psum | solution.py:11
  541.1 3.8 convolution_bitcast_fusion
  545.0 216.1 %reduce-scatter.2.cloned.1.call-done = f32[32,256]{1,0:T(8,128)} async-done(((f32[1024,256]{1,0:T(8,128)}), f32[32,256]{1,0:T(8,128)}) %reduce-scatter.2.cloned.1.call-update) | async-done | bytes 32784 | tf_op jit(solution)/shard_map/reduce_scatter | solution.py:34
  761.1 1.9 fusion.8
  763.1 273.3 %all-reduce.10.cloned.1.call-done = f32[256,256]{1,0:T(8,128)} async-done(((f32[256,256]{1,0:T(8,128)}), f32[256,256]{1,0:T(8,128)}) %all-reduce.10.cloned.1.call-update) | async-done | bytes 262160 | tf_op jit(solution)/shard_map/psum | solution.py:35
  1036.4 1.8 fusion
  1038.3 75.7 %all-gather.5.cloned.1.call-done = f32[1024,256]{1,0:T(8,128)} async-done(((f32[32,256]{1,0:T(8,128)}), f32[1024,256]{1,0:T(8,128)}) %all-gather.5.cloned.1.call-update) | async-done | bytes 1048592 | tf_op jit(solution)/shard_map/all_gather | solution.py:37
  1114.0 1.9 dynamic-slice_select_fusion
  1115.9 117.1 %all-reduce.12.cloned.1.call-done = f32[512,256]{1,0:T(8,128)} async-done(((f32[512,256]{1,0:T(8,128)}), f32[512,256]{1,0:T(8,128)}) %all-reduce.12.cloned.1.call-update) | async-done | bytes 524304 | tf_op jit(solution)/shard_map/psum | solution.py:11
  1233.0 3.0 fusion.15
  1236.0 3.4 subtract_select_fusion
  (45 shorter events, 4.0 us)
Async XLA Ops:
  6.5 278.6 %all-reduce.6.cloned.1.call-start = ((), (), s32[]{:S(2)}) async-start(), calls=%async_computation.1 | async-start | bytes 524288 | tf_op jit(solution)/shard_map/psum | solution.py:26
  8.5 338.2 %copy-start.4 = (f32[32,256]{1,0:T(8,128)S(1)}, f32[32,256]{1,0:T(8,128)}, u32[]{:S(2)}) copy-start(f32[32,256]{1,0:T(8,128)} %param.3) | copy-start | bytes 98308
  8.5 413.6 %all-gather.3.cloned.1.call-start = ((), (), s32[]{:S(2)}) async-start(), calls=%async_computation.2 | async-start | bytes 1081344 | tf_op jit(solution)/shard_map/all_gather | solution.py:29
  308.8 232.3 %copy-start = (f32[1024,512]{1,0:T(8,128)S(1)}, f32[1024,512]{1,0:T(8,128)}, u32[]{:S(2)}) copy-start(f32[1024,512]{1,0:T(8,128)} %param.2) | copy-start | bytes 6291460
  347.9 193.2 %all-reduce.8.cloned.1.call-start = ((), (), s32[]{:S(2)}) async-start(), calls=%async_computation.3 | async-start | bytes 1048576 | tf_op jit(solution)/shard_map/psum | solution.py:11
  424.0 337.1 %reduce-scatter.2.cloned.1.call-start = ((), (), s32[]{:S(2)}) async-start(), calls=%async_computation.4 | async-start | bytes 1081344 | tf_op jit(solution)/shard_map/reduce_scatter | solution.py:34
  545.0 688.0 %copy-start.1 = (f32[1024,256]{1,0:T(8,128)S(1)}, f32[1024,256]{1,0:T(8,128)}, u32[]{:S(2)}) copy-start(f32[1024,256]{1,0:T(8,128)} %all-gather.3.cloned.1.call-done) | copy-start | bytes 3145732
  545.0 491.4 %all-reduce.10.cloned.1.call-start = ((), (), s32[]{:S(2)}) async-start(), calls=%async_computation.5 | async-start | bytes 524288 | tf_op jit(solution)/shard_map/psum | solution.py:35
  763.0 350.9 %all-gather.5.cloned.1.call-start = ((), (), s32[]{:S(2)}) async-start(), calls=%async_computation.6 | async-start | bytes 1081344 | tf_op jit(solution)/shard_map/all_gather | solution.py:37
  1038.2 194.7 %all-reduce.12.cloned.1.call-start = ((), (), s32[]{:S(2)}) async-start(), calls=%async_computation.7 | async-start | bytes 1048576 | tf_op jit(solution)/shard_map/psum | solution.py:11
  1233.0 3.0 copy-start.2
  1233.0 3.0 copy-start.3
Sparse Core Ops, SparseCore 0:
  12.3 272.7 all-reduce.5
  348.0 74.0 all-gather.2
  424.5 116.5 all-reduce.7
  545.4 215.7 reduce-scatter.1
  766.0 270.3 all-reduce.9
  1039.9 74.0 all-gather.4
  1116.4 116.5 all-reduce.11
where the time goes:
time: 1250 us
  waiting for transfers between devices  1150 us (92%)
  other arithmetic  59 us (5%)
  matrix products  16.9 us (1%)
  between operations  14.9 us (1%)
    psum x1, waiting for transfers between devices, on_device(): gram = lax.psum(mult(panel.T, panel), ('row', 'col'))  277 us
    psum x1, waiting for transfers between devices, on_device(): inner = lax.psum(mult(basis.T, product_part), ('row', 'col'))  273 us
    psum x2, waiting for transfers between devices, from_root(): return lax.psum(jnp.where(mine, x, jnp.zeros_like(x)), axis)  234 us
    reduce_scatter x1, waiting for transfers between devices, on_device(): lax.psum_scatter(mult(matrix, basis_c), 'col', scatter_dimension=0, tiled...  216 us
    all_gather x1, waiting for transfers between devices, on_device(): shifted_r = lax.all_gather(shifted_part, 'col', axis=0, tiled=True)  75.7 us
    all_gather x1, waiting for transfers between devices, on_device(): basis_r = lax.all_gather(basis, 'col', axis=0, tiled=True)  74.1 us
    another operation x6, other arithmetic, on_device(): factor = jnp.linalg.cholesky(gram)  33.9 us
  transfers between devices with their start and end apart: 7, of which 7 were waited for; matrix products, arithmetic and copies ran while one was open for 0% of the time, Pallas kernels for 0%

commit v1 on v0

v1 whole, which is shorter than its diff:
```python
import functools

import jax
import jax.numpy as jnp
from jax import lax
from jax.experimental import pallas as pl
from jax.experimental.pallas import tpu as pltpu
from jax.sharding import PartitionSpec as P

HIGH = lax.Precision.HIGHEST
MESH = pl.DeviceIdType.MESH
F32 = jnp.float32
NX, NZ, NR, NC = 4, 8, 16, 32
H = 32
B = 256
G16 = 16
P_Z, P_X, P_PERM, P_ROW = 0, 1, 4, 5
Z_RS, Z_PERM, Z_ROW, Z_Z, Z_X = 6, 7, 8, 9, 10
G_Z, G_X, G_ROW = 14, 15, 16
M_Z, M_X, M_ROW = 17, 18, 19
SEMS = 20


def nn(a, b):
    return jnp.dot(a, b, precision=HIGH, preferred_element_type=F32)


def nt(a, b):
    return lax.dot_general(a, b, (((1,), (1,)), ((), ())), precision=HIGH, preferred_element_type=F32)


def tn(a, b):
    return lax.dot_general(a, b, (((0,), (0,)), ((), ())), precision=HIGH, preferred_element_type=F32)


def kernel(a_hbm, p_ref, out_hbm, a_v, at_v, o_v, pr, zr, pc, pct, zc, zpart, zrs, gz, gx, gf, mz, mx, mf, w, blk, sub,
           xc, yc, send, recv, local):
    r = lax.axis_index("row")
    c = lax.axis_index("col")
    z = c // NX
    x = c % NX
    r2, c2 = c % NR, 2 * r + c // NR
    r1, c1 = c // 2, (c % 2) * NR + r
    alone = jnp.logical_and(r2 == r, c2 == c)

    def z_peer(d):
        return (r, lax.rem(z + d, NZ) * NX + x)

    def x_peer(d):
        return (r, z * NX + lax.rem(x + d, NX))

    def row_peer(d):
        return (lax.rem(r + d, NR), c)

    barrier = pltpu.get_barrier_semaphore()

    def greet(peer, count):
        def body(d, carry):
            pl.semaphore_signal(barrier, inc=1, device_id=peer(d), device_id_type=MESH)
            return carry
        lax.fori_loop(1, count, body, 0)

    greet(z_peer, NZ)
    greet(x_peer, NX)
    greet(row_peer, NR)

    @pl.when(jnp.logical_not(alone))
    def _():
        pl.semaphore_signal(barrier, inc=1, device_id=(r2, c2), device_id_type=MESH)
        pl.semaphore_signal(barrier, inc=1, device_id=(r1, c1), device_id_type=MESH)

    a_copy = pltpu.make_async_copy(a_hbm, a_v, local.at[0])
    a_copy.start()
    pl.semaphore_wait(barrier, NZ - 1 + NX - 1 + NR - 1 + jnp.where(alone, 0, 2))

    def fan(src, dst, peer, count, slot):
        def body(d, carry):
            pltpu.make_async_remote_copy(
                src_ref=src(d), dst_ref=dst(d), send_sem=send.at[slot], recv_sem=recv.at[slot],
                device_id=peer(d), device_id_type=MESH).start()
            return carry
        lax.fori_loop(1, count, body, 0)

    def landed(ref, slot):
        pltpu.make_async_copy(ref, ref, recv.at[slot]).wait()

    def left(ref, slot):
        pltpu.make_async_copy(ref, ref, send.at[slot]).wait()

    def fan_x(buf, slot):
        def body(d, carry):
            pltpu.make_async_remote_copy(
                src_ref=buf.at[:, x], dst_ref=buf.at[:, x], send_sem=send.at[slot + d - 1],
                recv_sem=recv.at[slot + d - 1], device_id=x_peer(d), device_id_type=MESH).start()
            return carry
        lax.fori_loop(1, NX, body, 0)

    def perm(src, dst_slot, dst_buf, device, slot):
        @pl.when(alone)
        def _():
            pltpu.make_async_copy(src, dst_slot(dst_buf), recv.at[slot]).start()

        @pl.when(jnp.logical_not(alone))
        def _():
            pltpu.make_async_remote_copy(
                src_ref=src, dst_ref=dst_slot(dst_buf), send_sem=send.at[slot], recv_sem=recv.at[slot],
                device_id=device, device_id_type=MESH).start()

    perm(p_ref, lambda b: b.at[r2], pc, (r2, c2), P_PERM)
    fan(lambda d: p_ref, lambda d: pr.at[z, x], z_peer, NZ, P_Z)
    pr[z, x] = p_ref[...]
    landed(pc.at[r], P_PERM)
    fan(lambda d: pc.at[r], lambda d: pc.at[r], row_peer, NR, P_ROW)

    a_copy.wait()

    def turn(lo, hi):
        def body(i, carry):
            tile = a_v[i].reshape(128, 512)
            at_v[i] = tile.T
            return carry
        lax.fori_loop(lo, hi, body, 0)

    turn(0, 4)
    landed(pr.at[0:NZ - 1, 0], P_Z)
    fan_x(pr, P_X)
    landed(pc.at[0:NR - 1], P_ROW)
    pct[...] = pc[...].reshape(NR * H, B).T

    def mine(cols):
        rows = pct[pl.ds(pl.multiple_of(r * G16, G16), G16), :]
        return nn(rows, cols[...].reshape(NR * H, B))

    gz[z] = mine(pc)
    fan(lambda d: gz.at[z], lambda d: gz.at[z], z_peer, NZ, G_Z)
    turn(4, 8)
    landed(gz.at[0:NZ - 1], G_Z)
    gx[x] = jnp.sum(gz[...], axis=0)
    fan(lambda d: gx.at[x], lambda d: gx.at[x], x_peer, NX, G_X)
    landed(gx.at[0:NX - 1], G_X)
    gf[r] = jnp.sum(gx[...], axis=0)
    fan(lambda d: gf.at[r], lambda d: gf.at[r], row_peer, NR, G_ROW)

    def arrived_x(buf, slot):
        for d in range(1, NX):
            landed(buf.at[:, 0], slot + d - 1)

    arrived_x(pr, P_X)

    def share(i, carry):
        total = jnp.zeros((256, B), F32)
        for k in range(NZ):
            total += nn(at_v[k, pl.ds(pl.multiple_of(i * 256, 256), 256), :], pr[k].reshape(128, B))
        zpart[pl.ds(i * 8, 8)] = total.reshape(8, H, B)
        return carry
    lax.fori_loop(0, 2, share, 0)
    zrs[r] = zpart[r]
    fan(lambda d: zpart.at[lax.rem(r + d, NR)], lambda d: zrs.at[r], row_peer, NR, Z_RS)

    landed(gf.at[0:NR - 1], G_ROW)
    w[...] = gf[...].reshape(B, B)
    lane = lax.broadcasted_iota(jnp.int32, (128, 128), 1)
    subl = lax.broadcasted_iota(jnp.int32, (128, 128), 0)

    def sweep(lo, hi):
        def body(k, a):
            in_col = lane == k
            in_row = subl == k
            col = jnp.sum(jnp.where(in_col, a, 0.0), axis=1, keepdims=True)
            row = jnp.sum(jnp.where(in_row, a, 0.0), axis=0, keepdims=True)
            piv = jnp.sum(jnp.where(lane[0:1] == k, row, 0.0), axis=1, keepdims=True)
            inv = 1.0 / piv
            scaled = row * inv
            other = a - col * scaled
            other = jnp.where(in_col, col * inv, other)
            return jnp.where(in_row, jnp.where(in_col, -inv, scaled), other)
        blk[...] = lax.fori_loop(lo, hi, body, blk[...])

    blk[...] = w[0:128, 0:128]
    sweep(0, 48)

    landed(zrs.at[0:NR - 1], Z_RS)
    zc[r] = jnp.sum(zrs[...], axis=0)
    perm(zc.at[r], lambda b: b.at[c1 // NX, c1 % NX], zr, (r1, c1), Z_PERM)
    fan(lambda d: zc.at[r], lambda d: zc.at[r], row_peer, NR, Z_ROW)
    sweep(48, 72)
    landed(zr.at[z, x], Z_PERM)
    fan(lambda d: zr.at[z, x], lambda d: zr.at[z, x], z_peer, NZ, Z_Z)
    sweep(72, 100)
    landed(zc.at[0:NR - 1], Z_ROW)
    mz[z] = mine(zc)
    fan(lambda d: mz.at[z], lambda d: mz.at[z], z_peer, NZ, M_Z)
    sweep(100, 128)
    landed(zr.at[0:NZ - 1, 0], Z_Z)
    fan_x(zr, Z_X)
    landed(mz.at[0:NZ - 1], M_Z)
    mx[x] = jnp.sum(mz[...], axis=0)
    fan(lambda d: mx.at[x], lambda d: mx.at[x], x_peer, NX, M_X)
    sub[...] = nn(w[128:256, 0:128], -blk[...])
    w[0:128, 0:128] = -blk[...]
    blk[...] = w[128:256, 128:256] - nt(sub[...], w[128:256, 0:128])
    landed(mx.at[0:NX - 1], M_X)
    mf[r] = jnp.sum(mx[...], axis=0)
    fan(lambda d: mf.at[r], lambda d: mf.at[r], row_peer, NR, M_ROW)
    sweep(0, 128)
    low = nn(blk[...], sub[...])
    w[128:256, 128:256] = -blk[...]
    w[128:256, 0:128] = low
    w[0:128, 128:256] = low.T
    w[0:128, 0:128] = w[0:128, 0:128] - tn(sub[...], low)
    yc[...] = nt(w[...], pc[...].reshape(NR * H, B))
    landed(mf.at[0:NR - 1], M_ROW)
    rest = nn(mf[...].reshape(B, B), yc[...])
    xc[...] = nt(w[...], zc[...].reshape(NR * H, B)) - nn(w[...], rest)

    def update(xx, d):
        change = nn(pr[:, xx].reshape(256, B), xc[...]) + nn(zr[:, xx].reshape(256, B), yc[...])
        t = lax.broadcasted_iota(jnp.int32, (256, 512), 0)
        rows = r * 1024 + (t // H) * (H * NX) + xx * H + t % H
        cols = c * 512 + lax.broadcasted_iota(jnp.int32, (256, 512), 1)
        old = a_v[:, xx].reshape(256, 512)
        o_v[:, xx] = jnp.where(rows >= cols, old - change, old).reshape(NZ, H, 512)
        pltpu.make_async_copy(o_v.at[:, xx], out_hbm.at[:, xx], local.at[1 + d]).start()

    update(x, 0)

    def tail(d, carry):
        landed(zr.at[:, 0], Z_X + d - 1)
        update(lax.rem(x - d + NX, NX), d)
        return carry
    lax.fori_loop(1, NX, tail, 0)

    for slot in (P_Z, Z_Z):
        left(pr.at[0:NZ - 1, 0], slot)
    for slot in (P_X, Z_X):
        for d in range(1, NX):
            left(pr.at[:, 0], slot + d - 1)
    for slot in (P_ROW, Z_RS, Z_ROW):
        left(pc.at[0:NR - 1], slot)
    for slot in (G_Z, M_Z):
        left(gz.at[0:NZ - 1], slot)
    for slot in (G_X, M_X):
        left(gx.at[0:NX - 1], slot)
    for slot in (G_ROW, M_ROW):
        left(gf.at[0:NR - 1], slot)

    @pl.when(jnp.logical_not(alone))
    def _():
        left(pc.at[0], P_PERM)
        left(pc.at[0], Z_PERM)

    def close(d, carry):
        xx = lax.rem(x - d + NX, NX)
        pltpu.make_async_copy(o_v.at[:, xx], out_hbm.at[:, xx], local.at[1 + d]).wait()
        return carry
    lax.fori_loop(0, NX, close, 0)


def on_device(matrix, panel):
    vm = lambda *s: pltpu.VMEM(s, F32)
    out = pl.pallas_call(
        kernel,
        out_shape=jax.ShapeDtypeStruct((NZ, NX, H, 512), F32),
        in_specs=[pl.BlockSpec(memory_space=pl.ANY), pl.BlockSpec(memory_space=pltpu.VMEM)],
        out_specs=pl.BlockSpec(memory_space=pl.ANY),
        scratch_shapes=[
            vm(NZ, NX, H, 512), vm(NZ, 512, 128), vm(NZ, NX, H, 512),
            vm(NZ, NX, H, B), vm(NZ, NX, H, B), vm(NR, H, B), vm(B, NR * H), vm(NR, H, B),
            vm(NR, H, B), vm(NR, H, B),
            vm(NZ, G16, B), vm(NX, G16, B), vm(NR, G16, B),
            vm(NZ, G16, B), vm(NX, G16, B), vm(NR, G16, B),
            vm(B, B), vm(128, 128), vm(128, 128), vm(B, 512), vm(B, 512),
            pltpu.SemaphoreType.DMA((SEMS,)), pltpu.SemaphoreType.DMA((SEMS,)), pltpu.SemaphoreType.DMA((5,)),
        ],
        compiler_params=pltpu.CompilerParams(
            collective_id=0, has_side_effects=True, vmem_limit_bytes=48 * 1024 * 1024),
        cost_estimate=pl.CostEstimate(flops=8 * 10**9, bytes_accessed=8 * 2**20, transcendentals=0),
    )(matrix.reshape(NZ, NX, H, 512), panel)
    return out.reshape(1024, 512)


def solution(mesh):
    return jax.shard_map(
        on_device,
        mesh=mesh,
        in_specs=(P("row", "col"), P(("row", "col"), None)),
        out_specs=P("row", "col"),
        check_vma=False,
    )
```

time: 1250 us -> 126 us (0.10)
  waiting for transfers between devices: 1150 us -> 0 us
  Pallas kernels: 0 us -> 122 us
  other arithmetic: 59 us -> 0 us
  matrix products: 16.9 us -> 0 us
  between operations: 14.9 us -> 0.01 us
    psum x4 -> x0, waiting for transfers between devices: 784 us -> none  [the longest x1 277 us: on_device(): gram = lax.psum(mult(panel.T, panel), ('row', 'col'))]
    reduce_scatter x1 -> x0, waiting for transfers between devices: 216 us -> none  [on_device(): lax.psum_scatter(mult(matrix, basis_c), 'col', scatter_dimension=0, tiled...]
    all_gather x2 -> x0, waiting for transfers between devices: 150 us -> none  [the longest x1 75.7 us: on_device(): shifted_r = lax.all_gather(shifted_part, 'col', axis=0, tiled=True)]
    pallas_call x0 -> x1, Pallas kernels: none -> 122 us  [on_device(): pl.pallas_call(kernel, out_shape=jax.ShapeDtypeStruct((NZ, NX, H, 512), F...]
    another operation x9 -> x0, other arithmetic: 53.7 us -> none  [the longest x6 33.9 us: on_device(): factor = jnp.linalg.cholesky(gram)]
    dot_general x6 -> x0, matrix products: 15.9 us -> none  [mult(): jnp.dot(left, right, precision=HIGH, preferred_element_type=jnp.float32)]
  transfers between devices with their start and end apart: 7 -> 0, of which waited for: 7 -> 0; matrix products, arithmetic and copies ran while one was open for 0% -> 0% of each run, Pallas kernels for 0% -> 0%
where the time goes in v1:
time: 126 us; the launch traced here: 125 us
  Pallas kernels  122 us (97%)
  local copies, waits for them, and re-layouts  3.67 us (3%)
    pallas_call x1, Pallas kernels, on_device(): pl.pallas_call(kernel, out_shape=jax.ShapeDtypeStruct((NZ, NX, H, 512), F...  122 us
    unnamed x5, local copies, waits for them, and re-layouts  3.67 us

profile of v1, /device:TPU:1, one launch (start us, length us, event | category | flops | bytes accessed | tf_op | source)
XLA Modules:
  0.0 125.3 jit_solution(6237792856803500487)
XLA Ops:
  0.0 0.0 copy-start
  0.0 1.6 %copy-done = f32[1024,512]{1,0:T(8,128)S(1)} copy-done((f32[1024,512]{1,0:T(8,128)S(1)}, f32[1024,512]{1,0:T(8,128)}, u32[]{:S(2)}) %copy-start) | copy-done | bytes 2097176
  1.6 0.0 copy-start.1
  1.6 0.8 copy-done.1
  2.4 121.6 %shard_map.28 = f32[8,4,32,512]{3,2,1,0:T(8,128)S(1)} custom-call(f32[8,4,32,512]{3,2,1,0:T(8,128)S(1)} %bitcast.3, f32[32,256]{1,0:T(8,128)S(1)} %copy-done.1), custom_call_target="tpu_custom_call" | custom-call | flops 8000000000 | bytes 8388608 | tf_op jit(solution)/shard_map/pallas_call | solution.py:261
  124.0 1.3 %copy.4 = f32[1024,512]{1,0:T(8,128)} copy(f32[1024,512]{1,0:T(8,128)S(1)} %bitcast.2) | data formatting | bytes 4194304
Async XLA Ops:
  0.0 1.6 %copy-start = (f32[1024,512]{1,0:T(8,128)S(1)}, f32[1024,512]{1,0:T(8,128)}, u32[]{:S(2)}) copy-start(f32[1024,512]{1,0:T(8,128)} %param.2) | copy-start | bytes 6291460
  1.6 0.8 copy-start.1

commit v2 on v0

v2 whole, which is shorter than its diff:
```python
import jax
import jax.numpy as jnp
from jax import lax
from jax.experimental import pallas as pl
from jax.experimental.pallas import tpu as pltpu
from jax.sharding import PartitionSpec as P

HIGH = lax.Precision.HIGHEST
MESH = pl.DeviceIdType.MESH
F32 = jnp.float32
NX, NY, NZ, NR = 4, 8, 8, 16
H = 32
B = 256
G16 = 16
P_Z, P_X, Z_Z, Z_X = 0, 8, 16, 24
P_PERM, P_Y, P_CORE, Z_CORE, Z_Y, Z_PERM, ZC_Y, ZC_CORE = 32, 33, 34, 35, 36, 37, 38, 39
G_SUM, M_SUM = 40, 46
SEMS = 52


def nn(a, b):
    return jnp.dot(a, b, precision=HIGH, preferred_element_type=F32)


def nt(a, b):
    return lax.dot_general(a, b, (((1,), (1,)), ((), ())), precision=HIGH, preferred_element_type=F32)


def tn(a, b):
    return lax.dot_general(a, b, (((0,), (0,)), ((), ())), precision=HIGH, preferred_element_type=F32)


def kernel(a_hbm, p_hbm, out_hbm, a_v, at_v, o_v, pv, pr, zr, pc, pct, zc, zpart, zcb, zs, zyb,
           gpart, gcb, gs, gyb, gzb, gxb, gf, mpart, mcb, ms, myb, mzb, mxb, mf, w, blk, sub, xc, yc, send, recv, local):
    r = lax.axis_index("row")
    c = lax.axis_index("col")
    y = r // 2
    k = r % 2
    z = c // NX
    x = c % NX
    r2, c2 = c % NR, 2 * r + c // NR
    r1, c1 = c // 2, (c % 2) * NR + r
    alone = jnp.logical_and(r2 == r, c2 == c)
    sibling = (2 * y + 1 - k, c)

    def z_peer(d):
        return (r, (z + d) % NZ * NX + x)

    def x_peer(d):
        return (r, z * NX + (x + d) % NX)

    def y_peer(d):
        return ((y + d) % NY * 2 + k, c)

    def send_to(src, dst, device, out_slot, in_slot):
        pltpu.make_async_remote_copy(
            src_ref=src, dst_ref=dst, send_sem=send.at[out_slot], recv_sem=recv.at[in_slot],
            device_id=device, device_id_type=MESH).start()

    def loop(lo, hi, step):
        def body(d, carry):
            step(d)
            return carry
        lax.fori_loop(lo, hi, body, 0)

    def landed(ref, slot):
        pltpu.make_async_copy(ref, ref, recv.at[slot]).wait()

    def left(ref, slot):
        pltpu.make_async_copy(ref, ref, send.at[slot]).wait()

    barrier = pltpu.get_barrier_semaphore()

    def greet(device):
        pl.semaphore_signal(barrier, inc=1, device_id=device, device_id_type=MESH)

    loop(1, NZ, lambda d: greet(z_peer(d)))
    loop(1, NX, lambda d: greet(x_peer(d)))
    loop(1, NY, lambda d: greet(y_peer(d)))
    greet(sibling)

    @pl.when(jnp.logical_not(alone))
    def _():
        greet((r2, c2))
        greet((r1, c1))

    p_copy = pltpu.make_async_copy(p_hbm, pv, local.at[4])
    a_copy = pltpu.make_async_copy(a_hbm, a_v, local.at[0])
    p_copy.start()
    a_copy.start()
    p_copy.wait()
    pr[z, x] = pv[...]
    gpart[...] = tn(pv[...], pv[...]).reshape(NY, 2, G16, B)
    pl.semaphore_wait(barrier, NZ - 1 + NX - 1 + NY - 1 + 1 + jnp.where(alone, 0, 2))

    def perm(src, dst, device, slot):
        @pl.when(alone)
        def _():
            pltpu.make_async_copy(src, dst, recv.at[slot]).start()

        @pl.when(jnp.logical_not(alone))
        def _():
            send_to(src, dst, device, slot, slot)

    def order(j):
        return jnp.where(j % 2 == 0, j // 2 + 1, NZ - 1 - j // 2)

    def gather_start(buf, zslot, xslot):
        loop(0, NZ - 1, lambda j: send_to(buf.at[z, x], buf.at[z, x], z_peer(order(j)), zslot, zslot + order(j)))
        loop(1, NX, lambda e: send_to(buf.at[z, x], buf.at[z, x], x_peer(e), xslot, xslot))

    def gather_forward(buf, zslot, xslot, lo, hi):
        def step(j):
            d = order(j)
            zz = (z - d + NZ) % NZ
            landed(buf.at[zz, x], zslot + d)
            loop(1, NX, lambda e: send_to(buf.at[zz, x], buf.at[zz, x], x_peer(e), xslot, xslot + d))
        loop(lo, hi, step)

    def gather_wait(buf, xslot, g):
        for i in range(2):
            zz = 2 * g + i
            landed(buf.at[0, 0:NX - 1], xslot + (z - zz + NZ) % NZ)

    def group(i):
        return (z // 2 + jnp.where(i == 2, 3, jnp.where(i == 3, 2, i))) % 4

    def to_row(buf, slot):
        loop(1, NY, lambda d: send_to(buf.at[y, k], buf.at[y, k], y_peer(d), slot, slot))

    def to_sibling(buf, slot):
        send_to(buf.at[:, k], buf.at[:, k], sibling, slot, slot)

    def sum_core(part, cb, slot):
        send_to(part.at[:, 1 - k], cb, sibling, slot, slot)

    def sum_y(part, cb, sb, yb, slot, into):
        landed(cb, slot)
        sb[...] = part[:, k] + cb[...]
        yb[y] = sb[y]
        loop(1, NY, lambda d: send_to(sb.at[(y + d) % NY], yb.at[y], y_peer(d), into, into))

    def sum_z(yb, zb, slot):
        landed(yb.at[0:NY - 1], slot + 1)
        zb[z] = jnp.sum(yb[...], axis=0)
        loop(1, NZ, lambda d: send_to(zb.at[z], zb.at[z], z_peer(d), slot + 2, slot + 2))

    def sum_x(zb, xb, slot):
        landed(zb.at[0:NZ - 1], slot + 2)
        xb[x] = jnp.sum(zb[...], axis=0)
        loop(1, NX, lambda d: send_to(xb.at[x], xb.at[x], x_peer(d), slot + 3, slot + 3))

    def sum_back_y(xb, full, slot):
        landed(xb.at[0:NX - 1], slot + 3)
        full[y, k] = jnp.sum(xb[...], axis=0)
        to_row(full, slot + 4)

    def sum_back_core(full, slot):
        landed(full.at[0:NY - 1, 0], slot + 4)
        to_sibling(full, slot + 5)

    def sum_end(full, slot):
        landed(full.at[:, 0], slot + 5)

    def turn(g):
        at_v[g] = a_v[pl.ds(2 * g, 2)].reshape(256, 512).T

    perm(pv, pc.at[r2 // 2, r2 % 2], (r2, c2), P_PERM)
    gather_start(pr, P_Z, P_X)
    sum_core(gpart, gcb, G_SUM)
    a_copy.wait()
    turn(0)
    gather_forward(pr, P_Z, P_X, 0, 2)
    sum_y(gpart, gcb, gs, gyb, G_SUM, G_SUM + 1)
    gather_forward(pr, P_Z, P_X, 2, 4)
    landed(pc.at[0, 0], P_PERM)
    to_row(pc, P_Y)
    gather_forward(pr, P_Z, P_X, 4, 7)
    turn(1)
    sum_z(gyb, gzb, G_SUM)
    loop(2, 4, turn)
    landed(pc.at[0:NY - 1, 0], P_Y)
    to_sibling(pc, P_CORE)
    sum_x(gzb, gxb, G_SUM)

    def share(i):
        g = group(i)
        gather_wait(pr, P_X, g)

        def half(h):
            rows = pl.ds(pl.multiple_of(h * 256, 256), 256)
            part = nn(at_v[g, rows, :], pr[pl.ds(2 * g, 2)].reshape(256, B)).reshape(4, 2, H, B)
            place = pl.ds(h * 4, 4)

            @pl.when(i == 0)
            def _():
                zpart[place] = part

            @pl.when(i > 0)
            def _():
                zpart[place] = zpart[place] + part
        loop(0, 2, half)
    loop(0, 4, share)
    send_to(zpart.at[:, 1 - k], zcb, sibling, Z_CORE, Z_CORE)
    landed(pc.at[:, 0], P_CORE)
    pct[...] = pc[...].reshape(NR * H, B).T
    mpart[...] = nn(pct[...], zpart[...].reshape(NR * H, B)).reshape(NY, 2, G16, B)
    sum_core(mpart, mcb, M_SUM)
    sum_back_y(gxb, gf, G_SUM)
    sum_y(zpart, zcb, zs, zyb, Z_CORE, Z_Y)
    sum_y(mpart, mcb, ms, myb, M_SUM, M_SUM + 1)
    sum_back_core(gf, G_SUM)

    lane = lax.broadcasted_iota(jnp.int32, (128, 128), 1)
    subl = lax.broadcasted_iota(jnp.int32, (128, 128), 0)

    def sweep(lo, hi):
        def body(j, a):
            in_col = lane == j
            in_row = subl == j
            col = jnp.sum(jnp.where(in_col, a, 0.0), axis=1, keepdims=True)
            row = jnp.sum(jnp.where(in_row, a, 0.0), axis=0, keepdims=True)
            piv = jnp.sum(jnp.where(lane[0:1] == j, row, 0.0), axis=1, keepdims=True)
            inv = 1.0 / piv
            scaled = row * inv
            other = a - col * scaled
            other = jnp.where(in_col, col * inv, other)
            return jnp.where(in_row, jnp.where(in_col, -inv, scaled), other)
        blk[...] = lax.fori_loop(lo, hi, body, blk[...])

    sum_end(gf, G_SUM)
    w[...] = gf[...].reshape(B, B)
    blk[...] = w[0:128, 0:128]
    sweep(0, 32)
    landed(zyb.at[0:NY - 1], Z_Y)
    zc[y, k] = jnp.sum(zyb[...], axis=0)
    perm(zc.at[y, k], zr.at[c1 // NX, c1 % NX], (r1, c1), Z_PERM)
    to_row(zc, ZC_Y)
    sum_z(myb, mzb, M_SUM)
    sweep(32, 64)
    landed(zr.at[0, 0], Z_PERM)
    gather_start(zr, Z_Z, Z_X)
    sweep(64, 80)
    gather_forward(zr, Z_Z, Z_X, 0, 2)
    sum_x(mzb, mxb, M_SUM)
    gather_forward(zr, Z_Z, Z_X, 2, 4)
    landed(zc.at[0:NY - 1, 0], ZC_Y)
    to_sibling(zc, ZC_CORE)
    sweep(80, 96)
    sum_back_y(mxb, mf, M_SUM)
    gather_forward(zr, Z_Z, Z_X, 4, 7)
    sweep(96, 128)
    sum_back_core(mf, M_SUM)
    sub[...] = nn(w[128:256, 0:128], -blk[...])
    w[0:128, 0:128] = -blk[...]
    blk[...] = w[128:256, 128:256] - nt(sub[...], w[128:256, 0:128])
    sweep(0, 128)
    low = nn(blk[...], sub[...])
    w[128:256, 128:256] = -blk[...]
    w[128:256, 0:128] = low
    w[0:128, 128:256] = low.T
    w[0:128, 0:128] = w[0:128, 0:128] - tn(sub[...], low)
    yc[...] = nt(w[...], pc[...].reshape(NR * H, B))
    sum_end(mf, M_SUM)
    rest = nn(mf[...].reshape(B, B), yc[...])
    landed(zc.at[:, 0], ZC_CORE)
    xc[...] = nt(w[...], zc[...].reshape(NR * H, B)) - nn(w[...], rest)

    def out_copy(g):
        place = pl.ds(2 * g, 2)
        return pltpu.make_async_copy(o_v.at[place], out_hbm.at[place], local.at[g])

    def update(i):
        g = group(i)
        gather_wait(zr, Z_X, g)
        place = pl.ds(2 * g, 2)
        change = nn(pr[place].reshape(256, B), xc[...]) + nn(zr[place].reshape(256, B), yc[...])
        rows = r * 1024 + g * 256 + lax.broadcasted_iota(jnp.int32, (256, 512), 0)
        cols = c * 512 + lax.broadcasted_iota(jnp.int32, (256, 512), 1)
        old = a_v[place].reshape(256, 512)
        o_v[place] = jnp.where(rows >= cols, old - change, old).reshape(2, NX, H, 512)
        out_copy(g).start()
    loop(0, 4, update)

    for slot in (P_Z, Z_Z):
        left(pr.at[0:NZ - 1, 0], slot)
    for slot in (P_X, Z_X):
        left(pr.at[:, 0:NX - 1], slot)
    for slot in (P_Y, Z_Y, ZC_Y):
        left(pc.at[0:NY - 1, 0], slot)
    for slot in (P_CORE, Z_CORE, ZC_CORE):
        left(pc.at[:, 0], slot)
    for slot in (G_SUM, M_SUM):
        left(gf.at[:, 0], slot)
        left(gf.at[0:NY - 1, 0], slot + 1)
        left(gf.at[0:NZ - 1, 0], slot + 2)
        left(gf.at[0:NX - 1, 0], slot + 3)
        left(gf.at[0:NY - 1, 0], slot + 4)
        left(gf.at[:, 0], slot + 5)

    @pl.when(jnp.logical_not(alone))
    def _():
        left(pc.at[0, 0], P_PERM)
        left(pc.at[0, 0], Z_PERM)

    loop(0, 4, lambda g: out_copy(g).wait())


def on_device(matrix, panel):
    vm = lambda *s: pltpu.VMEM(s, F32)
    sums = [vm(NY, 2, G16, B), vm(NY, G16, B), vm(NY, G16, B), vm(NY, G16, B), vm(NZ, G16, B), vm(NX, G16, B),
            vm(NY, 2, G16, B)]
    out = pl.pallas_call(
        kernel,
        out_shape=jax.ShapeDtypeStruct((NZ, NX, H, 512), F32),
        in_specs=[pl.BlockSpec(memory_space=pltpu.HBM), pl.BlockSpec(memory_space=pltpu.HBM)],
        out_specs=pl.BlockSpec(memory_space=pltpu.HBM),
        scratch_shapes=[
            vm(NZ, NX, H, 512), vm(4, 512, 256), vm(NZ, NX, H, 512), vm(H, B),
            vm(NZ, NX, H, B), vm(NZ, NX, H, B), vm(NY, 2, H, B), vm(B, NR * H), vm(NY, 2, H, B),
            vm(NY, 2, H, B), vm(NY, H, B), vm(NY, H, B), vm(NY, H, B),
            *sums, *sums,
            vm(B, B), vm(128, 128), vm(128, 128), vm(B, 512), vm(B, 512),
            pltpu.SemaphoreType.DMA((SEMS,)), pltpu.SemaphoreType.DMA((SEMS,)), pltpu.SemaphoreType.DMA((5,)),
        ],
        compiler_params=pltpu.CompilerParams(
            collective_id=0, has_side_effects=True, vmem_limit_bytes=60 * 1024 * 1024),
        cost_estimate=pl.CostEstimate(flops=8 * 10**9, bytes_accessed=8 * 2**20, transcendentals=0),
    )(matrix.reshape(NZ, NX, H, 512), panel)
    return out.reshape(1024, 512)


def solution(mesh):
    return jax.shard_map(
        on_device,
        mesh=mesh,
        in_specs=(P("row", "col"), P(("row", "col"), None)),
        out_specs=P("row", "col"),
        check_vma=False,
    )
```

time: 1250 us -> 104 us (0.08)
  waiting for transfers between devices: 1150 us -> 0 us
  Pallas kernels: 0 us -> 100 us
  other arithmetic: 59 us -> 0 us
  matrix products: 16.9 us -> 0 us
  between operations: 14.9 us -> 0.01 us
    psum x4 -> x0, waiting for transfers between devices: 784 us -> none  [the longest x1 277 us: on_device(): gram = lax.psum(mult(panel.T, panel), ('row', 'col'))]
    reduce_scatter x1 -> x0, waiting for transfers between devices: 216 us -> none  [on_device(): lax.psum_scatter(mult(matrix, basis_c), 'col', scatter_dimension=0, tiled...]
    all_gather x2 -> x0, waiting for transfers between devices: 150 us -> none  [the longest x1 75.7 us: on_device(): shifted_r = lax.all_gather(shifted_part, 'col', axis=0, tiled=True)]
    pallas_call x0 -> x1, Pallas kernels: none -> 100 us  [on_device(): pl.pallas_call(kernel, out_shape=jax.ShapeDtypeStruct((NZ, NX, H, 512), F...]
    another operation x9 -> x0, other arithmetic: 53.7 us -> none  [the longest x6 33.9 us: on_device(): factor = jnp.linalg.cholesky(gram)]
    dot_general x6 -> x0, matrix products: 15.9 us -> none  [mult(): jnp.dot(left, right, precision=HIGH, preferred_element_type=jnp.float32)]
  transfers between devices with their start and end apart: 7 -> 0, of which waited for: 7 -> 0; matrix products, arithmetic and copies ran while one was open for 0% -> 0% of each run, Pallas kernels for 0% -> 0%
where the time goes in v2:
time: 104 us; the launch traced here: 103 us
  Pallas kernels  100 us (96%)
  local copies, waits for them, and re-layouts  3.08 us (3%)
    pallas_call x1, Pallas kernels, on_device(): pl.pallas_call(kernel, out_shape=jax.ShapeDtypeStruct((NZ, NX, H, 512), F...  100 us
    unnamed x1, local copies, waits for them, and re-layouts  3.08 us

profile of v2, /device:TPU:1, one launch (start us, length us, event | category | flops | bytes accessed | tf_op | source)
XLA Modules:
  0.0 103.4 jit_solution(13323615134787943975)
XLA Ops:
  0.0 100.3 %shard_map.28 = f32[8,4,32,512]{3,2,1,0:T(8,128)} custom-call(f32[8,4,32,512]{3,2,1,0:T(8,128)} %bitcast.3, f32[32,256]{1,0:T(8,128)} %p_hbm.1), custom_call_target="tpu_custom_call" | custom-call | flops 8000000000 | bytes 8388608 | tf_op jit(solution)/shard_map/pallas_call | solution.py:313
  100.3 3.1 %copy.4 = f32[1024,512]{1,0:T(8,128)} copy(f32[1024,512]{1,0:T(8,128)} %bitcast.2) | data formatting | bytes 4194304

commit v3 on v2

--- a/solution.py
+++ b/solution.py
@@ -30,8 +30,19 @@
     return lax.dot_general(a, b, (((0,), (0,)), ((), ())), precision=HIGH, preferred_element_type=F32)
 
 
-def kernel(a_hbm, p_hbm, out_hbm, a_v, at_v, o_v, pv, pr, zr, pc, pct, zc, zpart, zcb, zs, zyb,
-           gpart, gcb, gs, gyb, gzb, gxb, gf, mpart, mcb, ms, myb, mzb, mxb, mf, w, blk, sub, xc, yc, send, recv, local):
+def split(a):
+    high = a.astype(jnp.bfloat16)
+    return high, (a - high.astype(F32)).astype(jnp.bfloat16)
+
+
+def three(a, b):
+    def one(u, v):
+        return jnp.dot(u, v, preferred_element_type=F32)
+    return one(a[0], b[0]) + (one(a[1], b[0]) + one(a[0], b[1]))
+
+
+def kernel(a_hbm, p_hbm, out_hbm, a_v, at_hi, at_lo, o_v, pv, pr, zr, pc, pct, zc, zpart, zcb, zs, zyb,
+           gpart, gcb, gs, gyb, gzb, gxb, gf, mpart, mcb, ms, myb, mzb, mxb, mf, w, blk, sub, xc, xh, xl, yc, yh, yl, send, recv, local):
     r = lax.axis_index("row")
     c = lax.axis_index("col")
     y = r // 2
@@ -163,11 +174,11 @@
         landed(full.at[:, 0], slot + 5)
 
     def turn(g):
-        at_v[g] = a_v[pl.ds(2 * g, 2)].reshape(256, 512).T
-
+        at_hi[g], at_lo[g] = split(a_v[pl.ds(2 * g, 2)].reshape(256, 512).T)
+
+    sum_core(gpart, gcb, G_SUM)
+    gather_start(pr, P_Z, P_X)
     perm(pv, pc.at[r2 // 2, r2 % 2], (r2, c2), P_PERM)
-    gather_start(pr, P_Z, P_X)
-    sum_core(gpart, gcb, G_SUM)
     a_copy.wait()
     turn(0)
     gather_forward(pr, P_Z, P_X, 0, 2)
@@ -181,15 +192,15 @@
     loop(2, 4, turn)
     landed(pc.at[0:NY - 1, 0], P_Y)
     to_sibling(pc, P_CORE)
-    sum_x(gzb, gxb, G_SUM)
 
     def share(i):
         g = group(i)
         gather_wait(pr, P_X, g)
+        panel = split(pr[pl.ds(2 * g, 2)].reshape(256, B))
 
         def half(h):
             rows = pl.ds(pl.multiple_of(h * 256, 256), 256)
-            part = nn(at_v[g, rows, :], pr[pl.ds(2 * g, 2)].reshape(256, B)).reshape(4, 2, H, B)
+            part = three((at_hi[g, rows, :], at_lo[g, rows, :]), panel).reshape(4, 2, H, B)
             place = pl.ds(h * 4, 4)
 
             @pl.when(i == 0)
@@ -200,71 +211,92 @@
             def _():
                 zpart[place] = zpart[place] + part
         loop(0, 2, half)
-    loop(0, 4, share)
+    loop(0, 2, share)
+    sum_x(gzb, gxb, G_SUM)
+    loop(2, 4, share)
     send_to(zpart.at[:, 1 - k], zcb, sibling, Z_CORE, Z_CORE)
     landed(pc.at[:, 0], P_CORE)
     pct[...] = pc[...].reshape(NR * H, B).T
+    sum_back_y(gxb, gf, G_SUM)
+    sum_y(zpart, zcb, zs, zyb, Z_CORE, Z_Y)
     mpart[...] = nn(pct[...], zpart[...].reshape(NR * H, B)).reshape(NY, 2, G16, B)
     sum_core(mpart, mcb, M_SUM)
-    sum_back_y(gxb, gf, G_SUM)
-    sum_y(zpart, zcb, zs, zyb, Z_CORE, Z_Y)
+    sum_back_core(gf, G_SUM)
     sum_y(mpart, mcb, ms, myb, M_SUM, M_SUM + 1)
-    sum_back_core(gf, G_SUM)
 
     lane = lax.broadcasted_iota(jnp.int32, (128, 128), 1)
     subl = lax.broadcasted_iota(jnp.int32, (128, 128), 0)
+    lane1 = lane[0:1]
+    subl1 = subl[:, 0:1]
 
     def sweep(lo, hi):
-        def body(j, a):
-            in_col = lane == j
-            in_row = subl == j
-            col = jnp.sum(jnp.where(in_col, a, 0.0), axis=1, keepdims=True)
-            row = jnp.sum(jnp.where(in_row, a, 0.0), axis=0, keepdims=True)
-            piv = jnp.sum(jnp.where(lane[0:1] == j, row, 0.0), axis=1, keepdims=True)
-            inv = 1.0 / piv
-            scaled = row * inv
-            other = a - col * scaled
-            other = jnp.where(in_col, col * inv, other)
-            return jnp.where(in_row, jnp.where(in_col, -inv, scaled), other)
+        def body(i, a):
+            j = 2 * i
+            c_0, c_1 = lane == j, lane == j + 1
+            r_0, r_1 = subl == j, subl == j + 1
+            col0 = jnp.sum(jnp.where(c_0, a, 0.0), axis=1, keepdims=True)
+            col1 = jnp.sum(jnp.where(c_1, a, 0.0), axis=1, keepdims=True)
+            row0 = jnp.sum(jnp.where(r_0, a, 0.0), axis=0, keepdims=True)
+            row1 = jnp.sum(jnp.where(r_1, a, 0.0), axis=0, keepdims=True)
+            p = jnp.sum(jnp.where(lane1 == j, row0, 0.0), axis=1, keepdims=True)
+            q = jnp.sum(jnp.where(lane1 == j + 1, row0, 0.0), axis=1, keepdims=True)
+            s = jnp.sum(jnp.where(lane1 == j + 1, row1, 0.0), axis=1, keepdims=True)
+            ip = 1.0 / p
+            t = q * ip
+            i11 = 1.0 / (s - q * t)
+            i01 = -t * i11
+            i00 = ip - t * i01
+            row0 = jnp.where(lane1 == j, -1.0, jnp.where(lane1 == j + 1, 0.0, row0))
+            row1 = jnp.where(lane1 == j, 0.0, jnp.where(lane1 == j + 1, -1.0, row1))
+            col0 = jnp.where(subl1 == j, -1.0, jnp.where(subl1 == j + 1, 0.0, col0))
+            col1 = jnp.where(subl1 == j, 0.0, jnp.where(subl1 == j + 1, -1.0, col1))
+            y0 = i00 * row0 + i01 * row1
+            y1 = i01 * row0 + i11 * row1
+            keep = jnp.where(c_0 | c_1 | r_0 | r_1, 0.0, a)
+            return keep - col0 * y0 - col1 * y1
         blk[...] = lax.fori_loop(lo, hi, body, blk[...])
 
     sum_end(gf, G_SUM)
     w[...] = gf[...].reshape(B, B)
     blk[...] = w[0:128, 0:128]
-    sweep(0, 32)
+    sweep(0, 14)
     landed(zyb.at[0:NY - 1], Z_Y)
     zc[y, k] = jnp.sum(zyb[...], axis=0)
     perm(zc.at[y, k], zr.at[c1 // NX, c1 % NX], (r1, c1), Z_PERM)
     to_row(zc, ZC_Y)
+    sweep(14, 18)
     sum_z(myb, mzb, M_SUM)
-    sweep(32, 64)
+    sweep(18, 40)
     landed(zr.at[0, 0], Z_PERM)
     gather_start(zr, Z_Z, Z_X)
-    sweep(64, 80)
+    sweep(40, 52)
     gather_forward(zr, Z_Z, Z_X, 0, 2)
     sum_x(mzb, mxb, M_SUM)
     gather_forward(zr, Z_Z, Z_X, 2, 4)
     landed(zc.at[0:NY - 1, 0], ZC_Y)
     to_sibling(zc, ZC_CORE)
-    sweep(80, 96)
+    sweep(52, 58)
     sum_back_y(mxb, mf, M_SUM)
     gather_forward(zr, Z_Z, Z_X, 4, 7)
-    sweep(96, 128)
-    sum_back_core(mf, M_SUM)
+    sweep(58, 64)
     sub[...] = nn(w[128:256, 0:128], -blk[...])
     w[0:128, 0:128] = -blk[...]
     blk[...] = w[128:256, 128:256] - nt(sub[...], w[128:256, 0:128])
-    sweep(0, 128)
+    sweep(0, 16)
+    sum_back_core(mf, M_SUM)
+    sweep(16, 64)
     low = nn(blk[...], sub[...])
     w[128:256, 128:256] = -blk[...]
     w[128:256, 0:128] = low
     w[0:128, 128:256] = low.T
     w[0:128, 0:128] = w[0:128, 0:128] - tn(sub[...], low)
     yc[...] = nt(w[...], pc[...].reshape(NR * H, B))
+    yh[...], yl[...] = split(yc[...])
     sum_end(mf, M_SUM)
     rest = nn(mf[...].reshape(B, B), yc[...])
     landed(zc.at[:, 0], ZC_CORE)
     xc[...] = nt(w[...], zc[...].reshape(NR * H, B)) - nn(w[...], rest)
+    xh[...], xl[...] = split(xc[...])
 
     def out_copy(g):
         place = pl.ds(2 * g, 2)
@@ -274,7 +306,8 @@
         g = group(i)
         gather_wait(zr, Z_X, g)
         place = pl.ds(2 * g, 2)
-        change = nn(pr[place].reshape(256, B), xc[...]) + nn(zr[place].reshape(256, B), yc[...])
+        change = three(split(pr[place].reshape(256, B)), (xh[...], xl[...]))
+        change += three(split(zr[place].reshape(256, B)), (yh[...], yl[...]))
         rows = r * 1024 + g * 256 + lax.broadcasted_iota(jnp.int32, (256, 512), 0)
         cols = c * 512 + lax.broadcasted_iota(jnp.int32, (256, 512), 1)
         old = a_v[place].reshape(256, 512)
@@ -308,6 +341,7 @@
 
 def on_device(matrix, panel):
     vm = lambda *s: pltpu.VMEM(s, F32)
+    bf = lambda *s: pltpu.VMEM(s, jnp.bfloat16)
     sums = [vm(NY, 2, G16, B), vm(NY, G16, B), vm(NY, G16, B), vm(NY, G16, B), vm(NZ, G16, B), vm(NX, G16, B),
             vm(NY, 2, G16, B)]
     out = pl.pallas_call(
@@ -316,15 +350,15 @@
         in_specs=[pl.BlockSpec(memory_space=pltpu.HBM), pl.BlockSpec(memory_space=pltpu.HBM)],
         out_specs=pl.BlockSpec(memory_space=pltpu.HBM),
         scratch_shapes=[
-            vm(NZ, NX, H, 512), vm(4, 512, 256), vm(NZ, NX, H, 512), vm(H, B),
+            vm(NZ, NX, H, 512), bf(4, 512, 256), bf(4, 512, 256), vm(NZ, NX, H, 512), vm(H, B),
             vm(NZ, NX, H, B), vm(NZ, NX, H, B), vm(NY, 2, H, B), vm(B, NR * H), vm(NY, 2, H, B),
             vm(NY, 2, H, B), vm(NY, H, B), vm(NY, H, B), vm(NY, H, B),
             *sums, *sums,
-            vm(B, B), vm(128, 128), vm(128, 128), vm(B, 512), vm(B, 512),
+            vm(B, B), vm(128, 128), vm(128, 128), vm(B, 512), bf(B, 512), bf(B, 512), vm(B, 512), bf(B, 512), bf(B, 512),
             pltpu.SemaphoreType.DMA((SEMS,)), pltpu.SemaphoreType.DMA((SEMS,)), pltpu.SemaphoreType.DMA((5,)),
         ],
         compiler_params=pltpu.CompilerParams(
-            collective_id=0, has_side_effects=True, vmem_limit_bytes=60 * 1024 * 1024),
+            collective_id=0, has_side_effects=True, vmem_limit_bytes=50 * 1024 * 1024),
         cost_estimate=pl.CostEstimate(flops=8 * 10**9, bytes_accessed=8 * 2**20, transcendentals=0),
     )(matrix.reshape(NZ, NX, H, 512), panel)
     return out.reshape(1024, 512)

time: 104 us -> 89 us (0.86)
  Pallas kernels: 100 us -> 86.8 us
    pallas_call x1, Pallas kernels: 100 us -> 86.8 us  [on_device(): pl.pallas_call(kernel, out_shape=jax.ShapeDtypeStruct((NZ, NX, H, 512), F...]
    unnamed x1 -> x3, local copies, waits for them, and re-layouts: 3.08 us -> 2.08 us
where the time goes in v3:
time: 89 us; the launch traced here: 88.9 us
  Pallas kernels  86.8 us (98%)
  local copies, waits for them, and re-layouts  2.08 us (2%)
    pallas_call x1, Pallas kernels, on_device(): pl.pallas_call(kernel, out_shape=jax.ShapeDtypeStruct((NZ, NX, H, 512), F...  86.8 us
    unnamed x3, local copies, waits for them, and re-layouts  2.08 us

profile of v3, /device:TPU:1, one launch (start us, length us, event | category | flops | bytes accessed | tf_op | source)
XLA Modules:
  0.0 88.9 jit_solution(2958345844069580081)
XLA Ops:
  0.0 0.0 copy-start
  0.0 0.8 copy-done
  0.8 86.8 %shard_map.28 = f32[8,4,32,512]{3,2,1,0:T(8,128)S(1)} custom-call(f32[8,4,32,512]{3,2,1,0:T(8,128)} %bitcast.3, f32[32,256]{1,0:T(8,128)S(1)} %copy-done), custom_call_target="tpu_custom_call" | custom-call | flops 8000000000 | bytes 8388608 | tf_op jit(solution)/shard_map/pallas_call | solution.py:347
  87.5 1.3 %copy.4 = f32[1024,512]{1,0:T(8,128)} copy(f32[1024,512]{1,0:T(8,128)S(1)} %bitcast.2) | data formatting | bytes 4194304
Async XLA Ops:
  0.0 0.8 copy-start

commit v4 on v3

--- a/solution.py
+++ b/solution.py
@@ -151,19 +151,19 @@
         yb[y] = sb[y]
         loop(1, NY, lambda d: send_to(sb.at[(y + d) % NY], yb.at[y], y_peer(d), into, into))
 
-    def sum_z(yb, zb, slot):
-        landed(yb.at[0:NY - 1], slot + 1)
-        zb[z] = jnp.sum(yb[...], axis=0)
+    def sum_z(src, count, came, zb, slot):
+        landed(src.at[0:count - 1], came)
+        zb[z] = jnp.sum(src[...], axis=0)
         loop(1, NZ, lambda d: send_to(zb.at[z], zb.at[z], z_peer(d), slot + 2, slot + 2))
 
-    def sum_x(zb, xb, slot):
-        landed(zb.at[0:NZ - 1], slot + 2)
-        xb[x] = jnp.sum(zb[...], axis=0)
+    def sum_x(src, count, came, xb, slot):
+        landed(src.at[0:count - 1], came)
+        xb[x] = jnp.sum(src[...], axis=0)
         loop(1, NX, lambda d: send_to(xb.at[x], xb.at[x], x_peer(d), slot + 3, slot + 3))
 
-    def sum_back_y(xb, full, slot):
-        landed(xb.at[0:NX - 1], slot + 3)
-        full[y, k] = jnp.sum(xb[...], axis=0)
+    def sum_back_y(src, count, came, full, slot):
+        landed(src.at[0:count - 1], came)
+        full[y, k] = jnp.sum(src[...], axis=0)
         to_row(full, slot + 4)
 
     def sum_back_core(full, slot):
@@ -188,7 +188,7 @@
     to_row(pc, P_Y)
     gather_forward(pr, P_Z, P_X, 4, 7)
     turn(1)
-    sum_z(gyb, gzb, G_SUM)
+    sum_z(gyb, NY, G_SUM + 1, gzb, G_SUM)
     loop(2, 4, turn)
     landed(pc.at[0:NY - 1, 0], P_Y)
     to_sibling(pc, P_CORE)
@@ -212,12 +212,12 @@
                 zpart[place] = zpart[place] + part
         loop(0, 2, half)
     loop(0, 2, share)
-    sum_x(gzb, gxb, G_SUM)
+    sum_x(gzb, NZ, G_SUM + 2, gxb, G_SUM)
     loop(2, 4, share)
     send_to(zpart.at[:, 1 - k], zcb, sibling, Z_CORE, Z_CORE)
     landed(pc.at[:, 0], P_CORE)
     pct[...] = pc[...].reshape(NR * H, B).T
-    sum_back_y(gxb, gf, G_SUM)
+    sum_back_y(gxb, NX, G_SUM + 3, gf, G_SUM)
     sum_y(zpart, zcb, zs, zyb, Z_CORE, Z_Y)
     mpart[...] = nn(pct[...], zpart[...].reshape(NR * H, B)).reshape(NY, 2, G16, B)
     sum_core(mpart, mcb, M_SUM)
@@ -229,62 +229,72 @@
     lane1 = lane[0:1]
     subl1 = subl[:, 0:1]
 
+    def pair(p, q, s):
+        ip = 1.0 / p
+        t = q * ip
+        i11 = 1.0 / (s - q * t)
+        i01 = -t * i11
+        return ip - t * i01, i01, i11
+
     def sweep(lo, hi):
-        def body(i, a):
-            j = 2 * i
-            c_0, c_1 = lane == j, lane == j + 1
-            r_0, r_1 = subl == j, subl == j + 1
-            col0 = jnp.sum(jnp.where(c_0, a, 0.0), axis=1, keepdims=True)
-            col1 = jnp.sum(jnp.where(c_1, a, 0.0), axis=1, keepdims=True)
-            row0 = jnp.sum(jnp.where(r_0, a, 0.0), axis=0, keepdims=True)
-            row1 = jnp.sum(jnp.where(r_1, a, 0.0), axis=0, keepdims=True)
-            p = jnp.sum(jnp.where(lane1 == j, row0, 0.0), axis=1, keepdims=True)
-            q = jnp.sum(jnp.where(lane1 == j + 1, row0, 0.0), axis=1, keepdims=True)
-            s = jnp.sum(jnp.where(lane1 == j + 1, row1, 0.0), axis=1, keepdims=True)
-            ip = 1.0 / p
-            t = q * ip
-            i11 = 1.0 / (s - q * t)
-            i01 = -t * i11
-            i00 = ip - t * i01
-            row0 = jnp.where(lane1 == j, -1.0, jnp.where(lane1 == j + 1, 0.0, row0))
-            row1 = jnp.where(lane1 == j, 0.0, jnp.where(lane1 == j + 1, -1.0, row1))
-            col0 = jnp.where(subl1 == j, -1.0, jnp.where(subl1 == j + 1, 0.0, col0))
-            col1 = jnp.where(subl1 == j, 0.0, jnp.where(subl1 == j + 1, -1.0, col1))
-            y0 = i00 * row0 + i01 * row1
-            y1 = i01 * row0 + i11 * row1
-            keep = jnp.where(c_0 | c_1 | r_0 | r_1, 0.0, a)
-            return keep - col0 * y0 - col1 * y1
-        blk[...] = lax.fori_loop(lo, hi, body, blk[...])
+        def step(i):
+            j = 4 * i
+            a = blk[...]
+            rows = [blk[pl.ds(j + u, 1), :] for u in range(4)]
+            cols = [jnp.sum(jnp.where(lane == j + u, a, 0.0), axis=1, keepdims=True) for u in range(4)]
+
+            def at(u, v):
+                return jnp.sum(jnp.where(lane1 == j + v, rows[u], 0.0), axis=1, keepdims=True)
+            e00, e01, e11 = pair(at(0, 0), at(0, 1), at(1, 1))
+            f00, f01, f10, f11 = at(0, 2), at(0, 3), at(1, 2), at(1, 3)
+            t00, t01 = e00 * f00 + e01 * f10, e00 * f01 + e01 * f11
+            t10, t11 = e01 * f00 + e11 * f10, e01 * f01 + e11 * f11
+            g00, g01, g11 = pair(at(2, 2) - f00 * t00 - f10 * t10, at(2, 3) - f00 * t01 - f10 * t11,
+                                 at(3, 3) - f01 * t01 - f11 * t11)
+            b00, b01 = -(t00 * g00 + t01 * g01), -(t00 * g01 + t01 * g11)
+            b10, b11 = -(t10 * g00 + t11 * g01), -(t10 * g01 + t11 * g11)
+            a00, a01 = e00 - b00 * t00 - b01 * t01, e01 - b00 * t10 - b01 * t11
+            a11 = e11 - b10 * t10 - b11 * t11
+            inverse = ((a00, a01, b00, b01), (a01, a11, b10, b11), (b00, b10, g00, g01), (b01, b11, g01, g11))
+            in_lane = (lane >= j) & (lane < j + 4)
+            in_subl = (subl >= j) & (subl < j + 4)
+            rows = [jnp.where(lane1 == j + u, -1.0, jnp.where(in_lane[0:1], 0.0, rows[u])) for u in range(4)]
+            cols = [jnp.where(subl1 == j + u, -1.0, jnp.where((subl1 >= j) & (subl1 < j + 4), 0.0, cols[u]))
+                    for u in range(4)]
+            new = jnp.where(in_lane | in_subl, 0.0, a)
+            for u in range(4):
+                m = inverse[u]
+                new -= cols[u] * (m[0] * rows[0] + m[1] * rows[1] + m[2] * rows[2] + m[3] * rows[3])
+            blk[...] = new
+        loop(lo, hi, step)
 
     sum_end(gf, G_SUM)
     w[...] = gf[...].reshape(B, B)
     blk[...] = w[0:128, 0:128]
-    sweep(0, 14)
+    sweep(0, 10)
     landed(zyb.at[0:NY - 1], Z_Y)
     zc[y, k] = jnp.sum(zyb[...], axis=0)
     perm(zc.at[y, k], zr.at[c1 // NX, c1 % NX], (r1, c1), Z_PERM)
     to_row(zc, ZC_Y)
-    sweep(14, 18)
-    sum_z(myb, mzb, M_SUM)
-    sweep(18, 40)
+    sweep(10, 13)
+    sum_x(myb, NY, M_SUM + 1, mxb, M_SUM)
+    sweep(13, 24)
+    sum_z(mxb, NX, M_SUM + 3, mzb, M_SUM)
+    sweep(24, 32)
     landed(zr.at[0, 0], Z_PERM)
     gather_start(zr, Z_Z, Z_X)
-    sweep(40, 52)
-    gather_forward(zr, Z_Z, Z_X, 0, 2)
-    sum_x(mzb, mxb, M_SUM)
-    gather_forward(zr, Z_Z, Z_X, 2, 4)
-    landed(zc.at[0:NY - 1, 0], ZC_Y)
-    to_sibling(zc, ZC_CORE)
-    sweep(52, 58)
-    sum_back_y(mxb, mf, M_SUM)
-    gather_forward(zr, Z_Z, Z_X, 4, 7)
-    sweep(58, 64)
     sub[...] = nn(w[128:256, 0:128], -blk[...])
     w[0:128, 0:128] = -blk[...]
     blk[...] = w[128:256, 128:256] - nt(sub[...], w[128:256, 0:128])
-    sweep(0, 16)
+    sweep(0, 7)
+    gather_forward(zr, Z_Z, Z_X, 0, 4)
+    landed(zc.at[0:NY - 1, 0], ZC_Y)
+    to_sibling(zc, ZC_CORE)
+    gather_forward(zr, Z_Z, Z_X, 4, 7)
+    sum_back_y(mzb, NZ, M_SUM + 2, mf, M_SUM)
+    sweep(7, 24)
     sum_back_core(mf, M_SUM)
-    sweep(16, 64)
+    sweep(24, 32)
     low = nn(blk[...], sub[...])
     w[128:256, 128:256] = -blk[...]
     w[128:256, 0:128] = low

time: 89 us -> 82.6 us (0.928)
  Pallas kernels: 86.8 us -> 80.3 us
    pallas_call x1, Pallas kernels: 86.8 us -> 80.3 us  [on_device(): pl.pallas_call(kernel, out_shape=jax.ShapeDtypeStruct((NZ, NX, H, 512), F...]
where the time goes in v4:
time: 82.6 us; the launch traced here: 82.4 us
  Pallas kernels  80.3 us (97%)
  local copies, waits for them, and re-layouts  2.08 us (3%)
    pallas_call x1, Pallas kernels, on_device(): pl.pallas_call(kernel, out_shape=jax.ShapeDtypeStruct((NZ, NX, H, 512), F...  80.3 us
    unnamed x3, local copies, waits for them, and re-layouts  2.08 us

profile of v4, /device:TPU:1, one launch (start us, length us, event | category | flops | bytes accessed | tf_op | source)
XLA Modules:
  0.0 82.4 jit_solution(14670588150812534804)
XLA Ops:
  0.0 0.0 copy-start
  0.0 0.8 copy-done
  0.8 80.3 %shard_map.28 = f32[8,4,32,512]{3,2,1,0:T(8,128)S(1)} custom-call(f32[8,4,32,512]{3,2,1,0:T(8,128)} %bitcast.3, f32[32,256]{1,0:T(8,128)S(1)} %copy-done), custom_call_target="tpu_custom_call" | custom-call | flops 8000000000 | bytes 8388608 | tf_op jit(solution)/shard_map/pallas_call | solution.py:357
  81.1 1.3 %copy.4 = f32[1024,512]{1,0:T(8,128)} copy(f32[1024,512]{1,0:T(8,128)S(1)} %bitcast.2) | data formatting | bytes 4194304
Async XLA Ops:
  0.0 0.8 copy-start

commit v5 on v4

--- a/solution.py
+++ b/solution.py
@@ -165,6 +165,22 @@
         landed(src.at[0:count - 1], came)
         full[y, k] = jnp.sum(src[...], axis=0)
         to_row(full, slot + 4)
+
+    def scatter_z(part, cb, sb, zb, slot):
+        landed(cb, slot)
+        sb[...] = part[:, k] + cb[...]
+        zb[z] = sb[z]
+        loop(1, NZ, lambda d: send_to(sb.at[(z + d) % NZ], zb.at[z], z_peer(d), slot + 1, slot + 1))
+
+    def middle_y(src, count, came, yb, slot):
+        landed(src.at[0:count - 1], came)
+        yb[y] = jnp.sum(src[...], axis=0)
+        loop(1, NY, lambda d: send_to(yb.at[y], yb.at[y], y_peer(d), slot + 2, slot + 2))
+
+    def back_z(src, count, came, full, slot):
+        landed(src.at[0:count - 1], came)
+        full[z, k] = jnp.sum(src[...], axis=0)
+        loop(1, NZ, lambda d: send_to(full.at[z, k], full.at[z, k], z_peer(d), slot + 4, slot + 4))
 
     def sum_back_core(full, slot):
         landed(full.at[0:NY - 1, 0], slot + 4)
@@ -211,18 +227,17 @@
             def _():
                 zpart[place] = zpart[place] + part
         loop(0, 2, half)
-    loop(0, 2, share)
     sum_x(gzb, NZ, G_SUM + 2, gxb, G_SUM)
-    loop(2, 4, share)
+    loop(0, 4, share)
     send_to(zpart.at[:, 1 - k], zcb, sibling, Z_CORE, Z_CORE)
+    sum_back_y(gxb, NX, G_SUM + 3, gf, G_SUM)
     landed(pc.at[:, 0], P_CORE)
     pct[...] = pc[...].reshape(NR * H, B).T
-    sum_back_y(gxb, NX, G_SUM + 3, gf, G_SUM)
     sum_y(zpart, zcb, zs, zyb, Z_CORE, Z_Y)
     mpart[...] = nn(pct[...], zpart[...].reshape(NR * H, B)).reshape(NY, 2, G16, B)
     sum_core(mpart, mcb, M_SUM)
     sum_back_core(gf, G_SUM)
-    sum_y(mpart, mcb, ms, myb, M_SUM, M_SUM + 1)
+    scatter_z(mpart, mcb, ms, mzb, M_SUM)
 
     lane = lax.broadcasted_iota(jnp.int32, (128, 128), 1)
     subl = lax.broadcasted_iota(jnp.int32, (128, 128), 0)
@@ -275,23 +290,23 @@
     landed(zyb.at[0:NY - 1], Z_Y)
     zc[y, k] = jnp.sum(zyb[...], axis=0)
     perm(zc.at[y, k], zr.at[c1 // NX, c1 % NX], (r1, c1), Z_PERM)
+    sum_x(mzb, NZ, M_SUM + 1, mxb, M_SUM)
+    sweep(10, 20)
+    middle_y(mxb, NX, M_SUM + 3, myb, M_SUM)
     to_row(zc, ZC_Y)
-    sweep(10, 13)
-    sum_x(myb, NY, M_SUM + 1, mxb, M_SUM)
-    sweep(13, 24)
-    sum_z(mxb, NX, M_SUM + 3, mzb, M_SUM)
-    sweep(24, 32)
+    sweep(20, 32)
     landed(zr.at[0, 0], Z_PERM)
     gather_start(zr, Z_Z, Z_X)
     sub[...] = nn(w[128:256, 0:128], -blk[...])
     w[0:128, 0:128] = -blk[...]
     blk[...] = w[128:256, 128:256] - nt(sub[...], w[128:256, 0:128])
     sweep(0, 7)
-    gather_forward(zr, Z_Z, Z_X, 0, 4)
+    gather_forward(zr, Z_Z, Z_X, 0, 2)
+    back_z(myb, NY, M_SUM + 2, mf, M_SUM)
+    gather_forward(zr, Z_Z, Z_X, 2, 4)
     landed(zc.at[0:NY - 1, 0], ZC_Y)
     to_sibling(zc, ZC_CORE)
     gather_forward(zr, Z_Z, Z_X, 4, 7)
-    sum_back_y(mzb, NZ, M_SUM + 2, mf, M_SUM)
     sweep(7, 24)
     sum_back_core(mf, M_SUM)
     sweep(24, 32)

time: 82.6 us -> 78.6 us (0.952)
  Pallas kernels: 80.3 us -> 76.2 us
    pallas_call x1, Pallas kernels: 80.3 us -> 76.2 us  [on_device(): pl.pallas_call(kernel, out_shape=jax.ShapeDtypeStruct((NZ, NX, H, 512), F...]
where the time goes in v5:
time: 78.6 us; the launch traced here: 78.3 us
  Pallas kernels  76.2 us (97%)
  local copies, waits for them, and re-layouts  2.08 us (3%)
    pallas_call x1, Pallas kernels, on_device(): pl.pallas_call(kernel, out_shape=jax.ShapeDtypeStruct((NZ, NX, H, 512), F...  76.2 us
    unnamed x3, local copies, waits for them, and re-layouts  2.08 us

profile of v5, /device:TPU:1, one launch (start us, length us, event | category | flops | bytes accessed | tf_op | source)
XLA Modules:
  0.0 78.3 jit_solution(7704234935556287643)
XLA Ops:
  0.0 0.0 copy-start
  0.0 0.8 copy-done
  0.8 76.2 %shard_map.28 = f32[8,4,32,512]{3,2,1,0:T(8,128)S(1)} custom-call(f32[8,4,32,512]{3,2,1,0:T(8,128)} %bitcast.3, f32[32,256]{1,0:T(8,128)S(1)} %copy-done), custom_call_target="tpu_custom_call" | custom-call | flops 8000000000 | bytes 8388608 | tf_op jit(solution)/shard_map/pallas_call | solution.py:372
  77.0 1.3 %copy.4 = f32[1024,512]{1,0:T(8,128)} copy(f32[1024,512]{1,0:T(8,128)S(1)} %bitcast.2) | data formatting | bytes 4194304
Async XLA Ops:
  0.0 0.8 copy-start

commit v6 on v5

--- a/solution.py
+++ b/solution.py
@@ -203,8 +203,8 @@
     landed(pc.at[0, 0], P_PERM)
     to_row(pc, P_Y)
     gather_forward(pr, P_Z, P_X, 4, 7)
+    sum_z(gyb, NY, G_SUM + 1, gzb, G_SUM)
     turn(1)
-    sum_z(gyb, NY, G_SUM + 1, gzb, G_SUM)
     loop(2, 4, turn)
     landed(pc.at[0:NY - 1, 0], P_Y)
     to_sibling(pc, P_CORE)

time: 78.6 us -> 78.6 us (level)
  no operation moved by 1% of the time
where the time goes in v6:
time: 78.6 us; the launch traced here: 78.2 us
  Pallas kernels  76.1 us (97%)
  local copies, waits for them, and re-layouts  2.08 us (3%)
    pallas_call x1, Pallas kernels, on_device(): pl.pallas_call(kernel, out_shape=jax.ShapeDtypeStruct((NZ, NX, H, 512), F...  76.1 us
    unnamed x3, local copies, waits for them, and re-layouts  2.08 us

profile of v6, /device:TPU:1, one launch (start us, length us, event | category | flops | bytes accessed | tf_op | source)
XLA Modules:
  0.0 78.2 jit_solution(3237250056640306669)
XLA Ops:
  0.0 0.0 copy-start
  0.0 0.8 copy-done
  0.8 76.1 %shard_map.28 = f32[8,4,32,512]{3,2,1,0:T(8,128)S(1)} custom-call(f32[8,4,32,512]{3,2,1,0:T(8,128)} %bitcast.3, f32[32,256]{1,0:T(8,128)S(1)} %copy-done), custom_call_target="tpu_custom_call" | custom-call | flops 8000000000 | bytes 8388608 | tf_op jit(solution)/shard_map/pallas_call | solution.py:372
  76.8 1.3 %copy.4 = f32[1024,512]{1,0:T(8,128)} copy(f32[1024,512]{1,0:T(8,128)S(1)} %bitcast.2) | data formatting | bytes 4194304
Async XLA Ops:
  0.0 0.8 copy-start
